TPU v7x, 32 devices: a whole 2x2x4 slice. The times are simulated.
32 devices in a mesh: walk: 16 (over z, y, x), elec: 2 (over core).
Axes of the slice: x: 2, y: 2, z: 4, core: 2. Of those that a mesh axis runs over, the one named last changes fastest.
Arguments:
- hidden: bfloat16 [32, 768, 256], P('walk', 'elec'), may hold values from -12 to 12
- w_query: bfloat16 [256, 256], replicated, may hold values from -0.375 to 0.375
- w_key: bfloat16 [256, 256], replicated, may hold values from -0.375 to 0.375
- w_value: bfloat16 [256, 256], replicated, may hold values from -0.375 to 0.375
- w_out: bfloat16 [256, 256], replicated, may hold values from -0.375 to 0.375
- neighbours: int32 [32, 6, 6], P('walk', 'elec'), may hold values from 0 to 5, as said below
- counts: int32 [32, 6], P('walk', 'elec'), may hold values from 2 to 6, as said below
- cotangent: bfloat16 [32, 768, 256], P('walk', 'elec'), may hold values from -6 to 6
Outputs:
- output: bfloat16 [32, 768, 256], P('walk', 'elec')
- grad_hidden: bfloat16 [32, 768, 256], P('walk', 'elec')
- grad_w_query: float32 [256, 256], replicated
- grad_w_key: float32 [256, 256], replicated
- grad_w_value: float32 [256, 256], replicated
- grad_w_out: float32 [256, 256], replicated
Inputs may be any that keep to these rules, and one draw needn't show every extreme that they name: neighbours[w, a, 0] is a itself; the 6 entries of a row are distinct blocks, each held by an index of elec within cyclic distance 1 of the index that holds block a; entries at and past counts[w, a] are ignored. In every draw all counts of the blocks of some index of elec equal 6.
All inputs are finite; a program needn't handle non-finite values.
Results may differ from a plain program's by a relative error of at most 0.012.
The roundings to bfloat16 on the way count: a program that leaves them out, or rounds other values in their place, can miss the bound.
Values may be sent and summed in bfloat16 or wider, within the bound.
A program may use at most 64 MiB of HBM per device.

v0:
```python
import jax
import jax.numpy as jnp
from jax import lax
from jax.sharding import PartitionSpec as P

HD = 64
BLOCK = 128


NEG_FILL = -1e30


def split_heads(array, head_count):
    return array.reshape(array.shape[:-1] + (head_count, array.shape[-1] // head_count))


def masked_scores(query_blk, key_slots, valid_keys, head_count, scaling):
    scores = (
        jnp.einsum(
            "bhd,khd->hbk",
            split_heads(query_blk, head_count),
            split_heads(key_slots, head_count),
            preferred_element_type=jnp.float32,
        )
        * scaling
    )
    return jnp.where(valid_keys[None, None, :], scores, NEG_FILL)


def body(hidden, w_query, w_key, w_value, w_out, neighbours, counts, cotangent):
    walk_dev, local_rows, model_width = hidden.shape
    blocks = neighbours.shape[1]
    slot_count = neighbours.shape[2]
    head_count = model_width // HD
    scaling = HD ** (-0.5)
    all_rows = hidden.reshape(-1, model_width)
    joined = jnp.concatenate([w_query, w_key, w_value], axis=1)
    projected = jnp.dot(all_rows, joined, preferred_element_type=jnp.float32).astype(jnp.bfloat16)
    query_rows = projected[:, :model_width]
    key_blocks = projected[:, model_width : 2 * model_width].reshape(
        walk_dev, blocks, BLOCK, model_width
    )
    value_blocks = projected[:, 2 * model_width :].reshape(walk_dev, blocks, BLOCK, model_width)
    cot_rows = cotangent.reshape(-1, model_width)
    d_attended = jnp.dot(cot_rows, w_out.T, preferred_element_type=jnp.float32).astype(jnp.bfloat16)
    key_store, value_store = (
        lax.all_gather(key_blocks, "elec", axis=1, tiled=True),
        lax.all_gather(value_blocks, "elec", axis=1, tiled=True),
    )
    stored = key_store.shape[1]
    walker_base = stored * jnp.arange(walk_dev, dtype=jnp.int32)[:, None, None]
    flat_slots = (neighbours + walker_base).reshape(-1, slot_count)
    key_flat = key_store.reshape(-1, BLOCK, model_width)
    value_flat = value_store.reshape(-1, BLOCK, model_width)
    query_items = query_rows.reshape(-1, BLOCK, model_width)
    count_items = counts.reshape(-1)
    grad_items = d_attended.reshape(-1, BLOCK, model_width)

    def slot_rows(flat_row, live_count):
        key_slots = jnp.take(key_flat, flat_row, axis=0).reshape(slot_count * BLOCK, model_width)
        value_slots = jnp.take(value_flat, flat_row, axis=0).reshape(
            slot_count * BLOCK, model_width
        )
        valid_keys = jnp.repeat(jnp.arange(slot_count, dtype=jnp.int32) < live_count, BLOCK)
        return (key_slots, value_slots, valid_keys)

    def forward_item(inputs):
        query_blk, flat_row, live_count = inputs
        key_slots, value_slots, valid_keys = slot_rows(flat_row, live_count)
        scores = masked_scores(query_blk, key_slots, valid_keys, head_count, scaling)
        row_max = jnp.max(scores, axis=-1, keepdims=True)
        log_total = row_max + jnp.log(jnp.sum(jnp.exp(scores - row_max), axis=-1, keepdims=True))
        weights = jnp.exp(scores - log_total).astype(jnp.bfloat16)
        attended = jnp.einsum(
            "hbk,khd->bhd",
            weights,
            split_heads(value_slots, head_count),
            preferred_element_type=jnp.float32,
        )
        return (attended.astype(jnp.bfloat16).reshape(BLOCK, model_width), log_total)

    attended_items, log_items = lax.map(forward_item, (query_items, flat_slots, count_items))
    attended_rows = attended_items.reshape(-1, model_width)
    output = (
        all_rows.astype(jnp.float32)
        + jnp.dot(attended_rows, w_out, preferred_element_type=jnp.float32)
    ).astype(jnp.bfloat16)
    walkers_all = walk_dev * lax.axis_size("walk")
    grad_out = jnp.dot(attended_rows.T, cot_rows, preferred_element_type=jnp.float32) / walkers_all

    def backward_item(inputs):
        query_blk, flat_row, live_count, attended_blk, log_total, grad_blk = inputs
        key_slots, value_slots, valid_keys = slot_rows(flat_row, live_count)
        scores = masked_scores(query_blk, key_slots, valid_keys, head_count, scaling)
        probabilities = jnp.exp(scores - log_total)
        weights = probabilities.astype(jnp.bfloat16)
        grad_heads = split_heads(grad_blk, head_count)
        d_weights = jnp.einsum(
            "bhd,khd->hbk",
            grad_heads,
            split_heads(value_slots, head_count),
            preferred_element_type=jnp.float32,
        )
        inner_sum = jnp.sum(
            grad_heads.astype(jnp.float32)
            * split_heads(attended_blk, head_count).astype(jnp.float32),
            axis=-1,
        ).T
        score_grad = (probabilities * (d_weights - inner_sum[..., None])).astype(jnp.bfloat16)
        d_query = (
            jnp.einsum(
                "hbk,khd->bhd",
                score_grad,
                split_heads(key_slots, head_count),
                preferred_element_type=jnp.float32,
            )
            * scaling
        )
        key_terms = (
            jnp.einsum(
                "hbk,bhd->khd",
                score_grad,
                split_heads(query_blk, head_count),
                preferred_element_type=jnp.float32,
            )
            * scaling
        )
        value_terms = jnp.einsum(
            "hbk,bhd->khd", weights, grad_heads, preferred_element_type=jnp.float32
        )
        return (
            d_query.astype(jnp.bfloat16).reshape(BLOCK, model_width),
            key_terms.reshape(-1, model_width),
            value_terms.reshape(-1, model_width),
        )

    query_grad_items, key_terms, value_terms = lax.map(
        backward_item, (query_items, flat_slots, count_items, attended_items, log_items, grad_items)
    )
    onehot = (
        neighbours.reshape(walk_dev, blocks * slot_count)[..., None]
        == jnp.arange(stored, dtype=jnp.int32)[None, None, :]
    ).astype(jnp.float32)

    def place(contribution):
        grouped = contribution.reshape(walk_dev, blocks * slot_count, BLOCK * model_width)
        placed = jnp.einsum("wsn,wsx->wnx", onehot, grouped, precision=lax.Precision.HIGHEST)
        return placed.reshape(walk_dev, stored, BLOCK, model_width).astype(jnp.bfloat16)

    key_round = place(key_terms)
    value_round = place(value_terms)
    key_wide = lax.optimization_barrier(key_round).astype(jnp.float32)
    value_wide = lax.optimization_barrier(value_round).astype(jnp.float32)
    key_sum, value_sum = (
        lax.psum_scatter(
            key_wide.astype(jnp.bfloat16), "elec", scatter_dimension=1, tiled=True
        ).astype(jnp.float32),
        lax.psum_scatter(
            value_wide.astype(jnp.bfloat16), "elec", scatter_dimension=1, tiled=True
        ).astype(jnp.float32),
    )
    key_grad_rows = key_sum.astype(jnp.bfloat16).reshape(-1, model_width)
    value_grad_rows = value_sum.astype(jnp.bfloat16).reshape(-1, model_width)
    query_grad_rows = query_grad_items.reshape(-1, model_width)
    grad_hidden = cot_rows.astype(jnp.float32) + jnp.dot(
        query_grad_rows, w_query.T, preferred_element_type=jnp.float32
    )
    grad_hidden = grad_hidden + jnp.dot(key_grad_rows, w_key.T, preferred_element_type=jnp.float32)
    grad_hidden = grad_hidden + jnp.dot(
        value_grad_rows, w_value.T, preferred_element_type=jnp.float32
    )
    grad_hidden = grad_hidden.astype(jnp.bfloat16).reshape(hidden.shape)
    grad_query = (
        jnp.dot(all_rows.T, query_grad_rows, preferred_element_type=jnp.float32) / walkers_all
    )
    grad_key = jnp.dot(all_rows.T, key_grad_rows, preferred_element_type=jnp.float32) / walkers_all
    grad_value = (
        jnp.dot(all_rows.T, value_grad_rows, preferred_element_type=jnp.float32) / walkers_all
    )
    grad_query, grad_key, grad_value, grad_out = lax.psum(
        (grad_query, grad_key, grad_value, grad_out), ("walk", "elec")
    )
    return (output.reshape(hidden.shape), grad_hidden, grad_query, grad_key, grad_value, grad_out)


def solution(mesh):
    placed = (
        P("walk", "elec", None),
        P(),
        P(),
        P(),
        P(),
        P("walk", "elec", None),
        P("walk", "elec"),
        P("walk", "elec", None),
    )
    return jax.shard_map(
        body,
        mesh=mesh,
        in_specs=placed,
        out_specs=(P("walk", "elec", None), P("walk", "elec", None), P(), P(), P(), P()),
        check_vma=False,
    )
```

profile of v0, /device:TPU:0, one launch (start us, length us, event | category | flops | bytes accessed | tf_op | source)
XLA Modules:
  0.0 324.3 jit_solution(6767902135031947009)
XLA Ops:
  9.6 1.6 fusion.7
  11.3 0.9 copy.50
  12.2 2.4 all_gather.7
  14.6 2.5 all_gather.6
  17.1 50.1 %while.26 = (s32[]{:T(128)}, bf16[6,128,256]{1,2,0:T(8,128)(2,1)}, f32[6,4,128,1]{2,1,3,0:T(4,128)S(1)}, s32[6,6]{1,0:T(8,128)S(1)}, bf16[12,128,256]{2,1,0:T(8,...) while((s32[]{:T(128)}, bf16[6,128,256]{1,2,0:T(8,128)(2,1)}, ...), condition=%wide.region_3.5_spmd, body=%wide.region_0.4_spmd.sunk | while | flops 103842352 | bytes 12211989 | solution.py:82
  18.5 0.9 constant_dynamic-slice_fusion.10
  19.3 1.7 gather_fusion.1
  26.8 0.9 constant_dynamic-slice_fusion.10
  27.7 1.7 gather_fusion.1
  35.2 0.9 constant_dynamic-slice_fusion.10
  36.0 1.7 gather_fusion.1
  43.5 0.9 constant_dynamic-slice_fusion.10
  44.4 1.7 gather_fusion.1
  51.9 0.9 constant_dynamic-slice_fusion.10
  52.7 1.7 gather_fusion.1
  60.2 0.9 constant_dynamic-slice_fusion.10
  61.1 1.7 gather_fusion.1
  67.5 70.7 %while.27 = (s32[]{:T(128)}, bf16[6,128,256]{2,1,0:T(8,128)(2,1)}, f32[6,768,256]{2,1,0:T(8,128)}, f32[6,768,256]{2,1,0:T(8,128)}, s32[6,6]{1,0:T(8,128)S(1)}, /...) while((s32[]{:T(128)}, bf16[6,128,256]{2,1,0:T(8,128)(2,1)}, ...), condition=%wide.region_6.8_spmd, body=%wide.region_4.7_spmd.sunk | while | flops 255197744 | bytes 26820472 | solution.py:137
  69.0 0.9 constant_dynamic-slice_fusion.13
  70.0 0.9 constant_dynamic-slice_fusion.11
  71.4 1.7 gather_fusion.2
  78.0 1.3 constant_dynamic-update-slice_fusion.9
  80.7 0.9 constant_dynamic-slice_fusion.13
  81.8 0.9 constant_dynamic-slice_fusion.11
  83.2 1.7 gather_fusion.2
  89.8 1.3 constant_dynamic-update-slice_fusion.9
  92.5 0.9 constant_dynamic-slice_fusion.13
  93.5 0.9 constant_dynamic-slice_fusion.11
  95.0 1.7 gather_fusion.2
  101.6 1.4 constant_dynamic-update-slice_fusion.9
  104.4 0.9 constant_dynamic-slice_fusion.13
  105.4 0.9 constant_dynamic-slice_fusion.11
  106.8 1.7 gather_fusion.2
  113.4 1.3 constant_dynamic-update-slice_fusion.9
  116.2 0.9 constant_dynamic-slice_fusion.13
  117.2 0.9 constant_dynamic-slice_fusion.11
  118.6 1.7 gather_fusion.2
  125.2 1.2 constant_dynamic-update-slice_fusion.9
  127.9 0.9 constant_dynamic-slice_fusion.13
  128.9 0.9 constant_dynamic-slice_fusion.11
  130.3 1.7 gather_fusion.2
  136.9 1.3 constant_dynamic-update-slice_fusion.9
  138.2 4.8 %reshape.165 = f32[2,18,32768]{2,1,0:T(8,128)} reshape(f32[6,768,256]{2,1,0:T(8,128)} %get-tuple-element.118) | data formatting | bytes 9437184 | tf_op jit(solution)/shard_map/reshape | solution.py:146
  143.0 5.0 %convolution_convert_fusion.1 = bf16[2,6,32768]{2,1,0:T(8,128)(2,1)S(1)} fusion(f32[2,18,32768]{2,1,0:T(8,128)} %reshape.165, s32[2,18]{1,0:T(2,128)S(1)} %eq.15), kind=kOutput, calls=%fused_computation.47 | convolution fusion | flops 85328088 | bytes 5505168 | tf_op jit(solution)/shard_map/wsn,wsx->wnx/dot_general | solution.py:147
  148.0 1.2 reshape.214
  149.2 0.9 copy.66
  150.4 4.8 %reshape.163 = f32[2,18,32768]{2,1,0:T(8,128)} reshape(f32[6,768,256]{2,1,0:T(8,128)} %get-tuple-element.117) | data formatting | bytes 9437184 | tf_op jit(solution)/shard_map/reshape | solution.py:146
  155.2 5.0 %convolution_convert_fusion.2 = bf16[2,6,32768]{2,1,0:T(8,128)(2,1)S(1)} fusion(f32[2,18,32768]{2,1,0:T(8,128)} %reshape.163, s32[2,18]{1,0:T(2,128)S(1)} %eq.15), kind=kOutput, calls=%fused_computation.48 | convolution fusion | flops 85328088 | bytes 5505168 | tf_op jit(solution)/shard_map/wsn,wsx->wnx/dot_general | solution.py:147
  160.2 1.2 reshape.213
  161.4 1.0 copy.65
  162.4 1.2 copy.51
  163.7 1.0 convolution_multiply_fusion.2
  164.7 1.0 fusion.12
  165.7 1.0 fusion.8
  167.1 1.0 copy.61
  168.1 1.0 fusion.10
  169.1 4.5 %reduce-scatter.3.cloned.1.call-done = bf16[2,3,128,256]{3,2,0,1:T(8,128)(2,1)} async-done(((bf16[2,6,128,256]{3,2,0,1:T(8,128)(2,1)}), bf16[2,3,128,256]{3,2,0,1:T(8,128)(2,1)}) %reduce-scatter.3.cloned.1.call-update) | async-done | bytes 393232 | tf_op jit(solution)/shard_map/reduce_scatter | solution.py:155
  173.6 1.0 copy.58
  174.7 1.0 fusion.11
  176.6 1.0 fusion.9
  177.6 134.0 %all-reduce.3.cloned.1.call-done = (f32[256,256]{0,1:T(8,128)}, f32[256,256]{0,1:T(8,128)}, f32[256,256]{0,1:T(8,128)}, f32[256,256]{1,0:T(8,128)}) async-done(((f32[256,256]{0,1:T(8,128)}, f32[256,256]{0,1:T(8,128)}, f32[256,256]{0,1:T(8,128)}, f32[256,256]{1,0:T(8,128)}), (f32[256,256]{0,1:T(8,128)}, f32[256,256]{0,1:T(8,128)}, f32[256,256]{0,1:T(8,128)}, ...) | async-done | bytes 1048592 | tf_op jit(solution)/shard_map/psum | solution.py:180
  311.6 1.8 copy.62
  313.4 1.8 copy.63
  315.2 1.8 copy.64
  (306 shorter events, 80.8 us)
Async XLA Ops:
  7.2 60.1 %copy-start = (bf16[256,256]{1,0:T(8,128)(2,1)S(1)}, bf16[256,256]{1,0:T(8,128)(2,1)}, u32[]{:S(2)}) copy-start(bf16[256,256]{1,0:T(8,128)(2,1)} %param.18) | copy-start | bytes 393220
  7.2 159.9 %reduce-scatter.5.cloned.1.call-start = ((), (), s32[]{:S(2)}) async-start(), calls=%async_computation.3 | async-start | bytes 1179648 | tf_op jit(solution)/shard_map/reduce_scatter | solution.py:158
  17.1 50.1 %copy-start.2 = (bf16[2,384,256]{2,1,0:T(8,128)(2,1)S(1)}, bf16[2,384,256]{2,1,0:T(8,128)(2,1)}, u32[]{:S(2)}) copy-start(bf16[2,384,256]{2,1,0:T(8,128)(2,1)} %param.21) | copy-start | bytes 1179652
  67.6 3.9 %copy-start.5 = (bf16[6,128,256]{2,1,0:T(8,128)(2,1)}, bf16[6,128,256]{2,1,0:T(8,128)(2,1)S(1)}, u32[]{:S(2)}) copy-start(bf16[6,128,256]{2,1,0:T(8,128)(2,1)S(1)} %get-tuple-element.470) | copy-start | bytes 1179652 | tf_op jit(solution)/shard_map/while
  78.0 1.3 copy-start.6
  79.3 3.9 %copy-start.5 = (bf16[6,128,256]{2,1,0:T(8,128)(2,1)}, bf16[6,128,256]{2,1,0:T(8,128)(2,1)S(1)}, u32[]{:S(2)}) copy-start(bf16[6,128,256]{2,1,0:T(8,128)(2,1)S(1)} %get-tuple-element.470) | copy-start | bytes 1179652 | tf_op jit(solution)/shard_map/while
  89.8 1.3 copy-start.6
  91.1 3.9 %copy-start.5 = (bf16[6,128,256]{2,1,0:T(8,128)(2,1)}, bf16[6,128,256]{2,1,0:T(8,128)(2,1)S(1)}, u32[]{:S(2)}) copy-start(bf16[6,128,256]{2,1,0:T(8,128)(2,1)S(1)} %get-tuple-element.470) | copy-start | bytes 1179652 | tf_op jit(solution)/shard_map/while
  101.6 1.4 copy-start.6
  103.0 3.9 %copy-start.5 = (bf16[6,128,256]{2,1,0:T(8,128)(2,1)}, bf16[6,128,256]{2,1,0:T(8,128)(2,1)S(1)}, u32[]{:S(2)}) copy-start(bf16[6,128,256]{2,1,0:T(8,128)(2,1)S(1)} %get-tuple-element.470) | copy-start | bytes 1179652 | tf_op jit(solution)/shard_map/while
  113.4 1.4 copy-start.6
  114.8 3.9 %copy-start.5 = (bf16[6,128,256]{2,1,0:T(8,128)(2,1)}, bf16[6,128,256]{2,1,0:T(8,128)(2,1)S(1)}, u32[]{:S(2)}) copy-start(bf16[6,128,256]{2,1,0:T(8,128)(2,1)S(1)} %get-tuple-element.470) | copy-start | bytes 1179652 | tf_op jit(solution)/shard_map/while
  125.2 1.3 copy-start.6
  126.5 3.9 %copy-start.5 = (bf16[6,128,256]{2,1,0:T(8,128)(2,1)}, bf16[6,128,256]{2,1,0:T(8,128)(2,1)S(1)}, u32[]{:S(2)}) copy-start(bf16[6,128,256]{2,1,0:T(8,128)(2,1)S(1)} %get-tuple-element.470) | copy-start | bytes 1179652 | tf_op jit(solution)/shard_map/while
  136.9 1.3 copy-start.6
  150.2 23.5 %reduce-scatter.3.cloned.1.call-start = ((), (), s32[]{:S(2)}) async-start(), calls=%async_computation.2 | async-start | bytes 1179648 | tf_op jit(solution)/shard_map/reduce_scatter | solution.py:155
  161.4 2.3 copy-start.3
  162.4 2.3 copy-start.1
  162.4 2.3 copy-start.4
  162.4 149.2 %all-reduce.3.cloned.1.call-start = ((), (), s32[]{:S(2)}) async-start(), calls=%async_computation.4 | async-start | bytes 2097152 | tf_op jit(solution)/shard_map/psum | solution.py:180
  163.7 3.0 copy-start.9
  169.1 6.6 %copy-start.8 = (bf16[256,256]{1,0:T(8,128)(2,1)S(1)}, bf16[256,256]{1,0:T(8,128)(2,1)}, u32[]{:S(2)}) copy-start(bf16[256,256]{1,0:T(8,128)(2,1)} %param.16) | copy-start | bytes 393220
  175.7 0.9 copy-start.10
  311.6 5.4 %copy-start.7 = (f32[256,256]{1,0:T(8,128)S(1)}, f32[256,256]{1,0:T(8,128)}, u32[]{:S(2)}) copy-start(f32[256,256]{1,0:T(8,128)} %get-tuple-element.479) | copy-start | bytes 786436
Sparse Core Ops, SparseCore 0:
  150.3 10.8 reduce-scatter.4
  163.5 10.0 reduce-scatter.2
  179.8 131.8 all-reduce.2
where the time goes:
time: 326 us; the launch traced here: 324 us
  waiting for transfers between devices  139 us (43%)
  local copies, waits for them, and re-layouts  116 us (36%)
  matrix products  35.7 us (11%)
  between operations  13.9 us (4%)
  other arithmetic  13.3 us (4%)
  blocking collectives  4.92 us (2%)
    psum x1, waiting for transfers between devices, body(): lax.psum((grad_query, grad_key, grad_value, grad_out), ('walk', 'elec'))  134 us
    dynamic_slice x42, local copies, waits for them, and re-layouts, body(): lax.map(forward_item, (query_items, flat_slots, count_items))  23.3 us
    gather x12, local copies, waits for them, and re-layouts, slot_rows(): jnp.take(value_flat, flat_row, axis=0)  20.4 us
    reshape x24, local copies, waits for them, and re-layouts, split_heads(): array.reshape(array.shape[:-1] + (head_count, array.shape[-1] // head_cou...  11.1 us
    dynamic_update_slice x18, local copies, waits for them, and re-layouts, body(): lax.map(backward_item, (query_items, flat_slots, count_items, attended_it...  11 us
    dot_general x2, matrix products, place(): jnp.einsum('wsn,wsx->wnx', onehot, grouped, precision=lax.Precision.HIGHEST)  10 us
    reshape x2, local copies, waits for them, and re-layouts, place(): contribution.reshape(walk_dev, blocks * slot_count, BLOCK * model_width)  9.53 us
    dynamic_update_slice x18, local copies, waits for them, and re-layouts, body(): lax.map(forward_item, (query_items, flat_slots, count_items))  8.3 us
  transfers between devices with their start and end apart: 3, of which 2 were waited for; matrix products, arithmetic and copies ran while one was open for 6% of the time, Pallas kernels for 0%

commit v1 on v0

--- a/solution.py
+++ b/solution.py
@@ -1,6 +1,8 @@
 import jax
 import jax.numpy as jnp
 from jax import lax
+from jax.experimental import pallas as pl
+from jax.experimental.pallas import tpu as pltpu
 from jax.sharding import PartitionSpec as P
 
 HD = 64
@@ -183,6 +185,249 @@
     return (output.reshape(hidden.shape), grad_hidden, grad_query, grad_key, grad_value, grad_out)
 
 
+F32 = jnp.float32
+BF16 = jnp.bfloat16
+PAIR = 2 * HD
+
+
+def dot_nn(a, b):
+    return lax.dot_general(a, b, (((1,), (0,)), ((), ())), preferred_element_type=F32)
+
+
+def dot_nt(a, b):
+    return lax.dot_general(a, b, (((1,), (1,)), ((), ())), preferred_element_type=F32)
+
+
+def by_head(block):
+    lane = lax.broadcasted_iota(jnp.int32, block.shape, 1)
+    zero = jnp.zeros_like(block)
+    return jnp.concatenate(
+        [jnp.where(lane < HD, block, zero), jnp.where(lane < HD, zero, block)], axis=0
+    )
+
+
+def walker_kernel(
+    nbr, cnt, hid, cot, wq, wk, wv, wo, out, grad, gw,
+    hs, cs, bs, bsend, q_s, k_s, v_s, da_s, kt_s, vt_s, dat_s,
+    at_s, att_s, dqt_s, dq_s, w_s, ds_s, qb_s, db_s, kp_s, vp_s, dk_s, dv_s, ht_s, osend, gsend,
+    send_sem, recv_sem, local_sem, osem_s, osem_r,
+):
+    e = lax.axis_index("elec")
+    other = 1 - e
+    blocks = hid.shape[1] // BLOCK
+    slots = nbr.shape[2]
+    n_blocks = 2 * blocks
+    half = hid.shape[1]
+    rows = 2 * half
+    pairs = hid.shape[2] // PAIR
+
+    barrier = pltpu.get_barrier_semaphore()
+    pl.semaphore_signal(barrier, inc=1, device_id={"elec": other}, device_id_type=pl.DeviceIdType.MESH)
+
+    lane = lax.broadcasted_iota(jnp.int32, (16, 128), 1)
+    sub = lax.broadcasted_iota(jnp.int32, (16, 128), 0)
+    for w in range(2):
+        bias = jnp.full((16, 128), NEG_FILL, F32)
+        for a in range(blocks):
+            for j in range(slots):
+                live = jnp.where(j < cnt[w, a], nbr[w, a, j], -1)
+                bias = jnp.where((sub == a) & (lane == live), 0.0, bias)
+        bsend[w] = bias.astype(BF16)
+
+    pl.semaphore_wait(barrier, 1)
+    sends = []
+    for i, (src, dst) in enumerate(((hid, hs), (cot, cs), (bsend, bs))):
+        copy = pltpu.make_async_remote_copy(
+            src_ref=src.at[other], dst_ref=dst.at[e], send_sem=send_sem.at[i], recv_sem=recv_sem.at[i],
+            device_id={"elec": other}, device_id_type=pl.DeviceIdType.MESH,
+        )
+        copy.start()
+        sends.append(copy)
+
+    hs[e] = hid[e]
+    cs[e] = cot[e]
+    bs[e] = bsend[e]
+
+    def project(h):
+        rows_h = hs[h]
+        q_s[h] = (dot_nn(rows_h, wq[...]).astype(BF16).astype(F32) * HD ** (-0.5)).astype(BF16)
+        k_s[h] = dot_nn(rows_h, wk[...]).astype(BF16)
+        v_s[h] = dot_nn(rows_h, wv[...]).astype(BF16)
+        da_s[h] = dot_nt(cs[h], wo[...]).astype(BF16)
+
+    project(e)
+    for copy in sends:
+        copy.wait()
+    project(other)
+
+    k_all = k_s[...].reshape(rows, -1)
+    v_all = v_s[...].reshape(rows, -1)
+    kt = k_all.T
+    vt = v_all.T
+    dat = da_s[...].reshape(rows, -1).T
+    which = (
+        lax.broadcasted_iota(jnp.int32, (rows, 128), 0) // BLOCK
+        == lax.broadcasted_iota(jnp.int32, (rows, 128), 1)
+    )
+    onehot = jnp.where(which, 1.0, 0.0).astype(BF16)
+    for p in range(pairs):
+        lanes = slice(p * PAIR, (p + 1) * PAIR)
+        kp_s[p, :, :PAIR] = k_all[:, lanes]
+        kp_s[p, :, PAIR:] = onehot
+        vp_s[p] = v_all[:, lanes]
+        kt_s[p] = kt[lanes]
+        vt_s[p] = vt[lanes]
+        for a in range(n_blocks):
+            dat_s[p, a] = dat[lanes, a * BLOCK : (a + 1) * BLOCK]
+            r = slice((a % blocks) * BLOCK, (a % blocks + 1) * BLOCK)
+            qb_s[p, a // blocks, a % blocks] = by_head(q_s[a // blocks, r, lanes])
+            db_s[p, a // blocks, a % blocks] = by_head(da_s[a // blocks, r, lanes])
+
+    def group(step, carry):
+        p = step // 2
+        g = step % 2
+        for i in range(blocks):
+            a = g * blocks + i
+            q2 = qb_s[p, g, i]
+            d2 = db_s[p, g, i]
+            bias = jnp.broadcast_to(bs[g, i : i + 1, :], (2 * BLOCK, 128))
+            scores = dot_nt(kp_s[p], jnp.concatenate([q2, bias], axis=1))
+            top = jnp.max(scores, axis=0, keepdims=True)
+            expo = jnp.exp(scores - top)
+            prob = expo * (1.0 / jnp.sum(expo, axis=0, keepdims=True))
+            weights = prob.astype(BF16)
+            cols = slice(i * 2 * BLOCK, (i + 1) * 2 * BLOCK)
+            w_s[:, cols] = weights
+            mixed = dot_nn(vt_s[p], weights)
+            att = jnp.concatenate([mixed[:HD, :BLOCK], mixed[HD:, BLOCK:]], axis=0).astype(BF16)
+            prod = att.astype(F32) * dat_s[p, a].astype(F32)
+            inner = jnp.concatenate(
+                [
+                    jnp.sum(prod[:HD], axis=0, keepdims=True),
+                    jnp.sum(prod[HD:], axis=0, keepdims=True),
+                ],
+                axis=1,
+            )
+            at_s[p, a] = att
+            att_s[p, g, i] = att.T
+            d_scores = (prob * (dot_nt(vp_s[p], d2) - inner)).astype(BF16)
+            ds_s[:, cols] = d_scores
+            mixed = dot_nn(kt_s[p], d_scores)
+            dqt = jnp.concatenate([mixed[:HD, :BLOCK], mixed[HD:, BLOCK:]], axis=0)
+            dqt = (dqt * HD ** (-0.5)).astype(BF16)
+            dqt_s[p, a] = dqt
+            dq_s[p, g, i] = dqt.T
+        dk_s[g, p] = dot_nn(ds_s[...], qb_s[p, g].reshape(-1, PAIR)).astype(BF16)
+        dv_s[g, p] = dot_nn(w_s[...], db_s[p, g].reshape(-1, PAIR)).astype(BF16)
+        return carry
+
+    lax.fori_loop(0, 2 * pairs, group, 0)
+
+    def whole(ref):
+        return jnp.concatenate([ref[p].reshape(rows, PAIR) for p in range(pairs)], axis=1)
+
+    h_all = hs[...].reshape(rows, -1)
+    c_all = cs[...].reshape(rows, -1)
+    ht = h_all.T
+    ht_s[...] = ht
+
+    def summed(ref):
+        return jnp.concatenate(
+            [(ref[0, p].astype(F32) + ref[1, p].astype(F32)).astype(BF16) for p in range(pairs)],
+            axis=1,
+        )
+
+    attended = whole(att_s)
+    d_query = whole(dq_s)
+    d_key = summed(dk_s)
+    d_value = summed(dv_s)
+    result = (h_all.astype(F32) + dot_nn(attended, wo[...])).astype(BF16)
+    osend[...] = result.reshape(osend.shape)
+    back = (
+        c_all.astype(F32)
+        + dot_nt(d_query, wq[...])
+        + dot_nt(d_key, wk[...])
+        + dot_nt(d_value, wv[...])
+    ).astype(BF16)
+    gsend[...] = back.reshape(gsend.shape)
+    sends = []
+    for i, (src, dst) in enumerate(((osend, out), (gsend, grad))):
+        copy = pltpu.make_async_remote_copy(
+            src_ref=src.at[other], dst_ref=dst.at[e], send_sem=osem_s.at[i], recv_sem=osem_r.at[i],
+            device_id={"elec": other}, device_id_type=pl.DeviceIdType.MESH,
+        )
+        copy.start()
+        sends.append(copy)
+    out[e] = osend[e]
+    grad[e] = gsend[e]
+    gw[0] = dot_nn(ht_s[...], d_query)
+    gw[1] = dot_nn(ht_s[...], d_key)
+    gw[2] = dot_nn(ht_s[...], d_value)
+    at = jnp.concatenate(
+        [
+            jnp.concatenate([at_s[p, a] for a in range(n_blocks)], axis=1)
+            for p in range(pairs)
+        ],
+        axis=0,
+    )
+    gw[3] = dot_nn(at, c_all)
+    for copy in sends:
+        copy.wait()
+
+
+def pair_body(hidden, w_query, w_key, w_value, w_out, neighbours, counts, cotangent):
+    half, width = hidden.shape[1:]
+    blocks = half // BLOCK
+    rows, pairs, n_blocks = 2 * half, width // PAIR, 2 * blocks
+    vmem = pl.BlockSpec(memory_space=pltpu.VMEM)
+    smem = pl.BlockSpec(memory_space=pltpu.SMEM)
+    both = (2, half, width)
+    by_pair = (pairs, 2, blocks, BLOCK, PAIR)
+    by_pair2 = (pairs, 2, blocks, 2 * BLOCK, PAIR)
+
+    def buf(*shape, dtype=BF16):
+        return pltpu.VMEM(shape, dtype)
+
+    out, grad, gw = pl.pallas_call(
+        walker_kernel,
+        out_shape=(
+            jax.ShapeDtypeStruct(hidden.shape, BF16),
+            jax.ShapeDtypeStruct(hidden.shape, BF16),
+            jax.ShapeDtypeStruct((4, width, width), F32),
+        ),
+        in_specs=[smem, smem] + [vmem] * 6,
+        out_specs=(vmem, vmem, vmem),
+        scratch_shapes=[
+            buf(*both), buf(*both), buf(2, 16, 128), buf(2, 16, 128),
+            buf(*both), buf(*both), buf(*both), buf(*both),
+            buf(pairs, PAIR, rows), buf(pairs, PAIR, rows), buf(pairs, n_blocks, PAIR, BLOCK),
+            buf(pairs, n_blocks, PAIR, BLOCK), buf(*by_pair),
+            buf(pairs, n_blocks, PAIR, BLOCK), buf(*by_pair),
+            buf(rows, blocks * 2 * BLOCK), buf(rows, blocks * 2 * BLOCK),
+            buf(*by_pair2), buf(*by_pair2),
+            buf(pairs, rows, 2 * PAIR), buf(pairs, rows, PAIR),
+            buf(2, pairs, rows, PAIR), buf(2, pairs, rows, PAIR),
+            buf(width, rows), buf(*both), buf(*both),
+            pltpu.SemaphoreType.DMA((3,)), pltpu.SemaphoreType.DMA((3,)),
+            pltpu.SemaphoreType.DMA((2,)),
+            pltpu.SemaphoreType.DMA((2,)), pltpu.SemaphoreType.DMA((2,)),
+        ],
+        compiler_params=pltpu.CompilerParams(
+            collective_id=0, has_side_effects=True, vmem_limit_bytes=48 * 1024 * 1024
+        ),
+    )(neighbours, counts, hidden, cotangent, w_query, w_key, w_value, w_out)
+    walkers_all = hidden.shape[0] * lax.axis_size("walk")
+    gw = lax.psum(gw, ("walk", "elec")) / walkers_all
+    return out, grad, gw[0], gw[1], gw[2], gw[3]
+
+
+def any_body(hidden, *rest):
+    blocks = rest[4].shape[1]
+    if lax.axis_size("elec") == 2 and hidden.shape[0] == 2 and 2 * blocks <= 128 and blocks <= 16:
+        return pair_body(hidden, *rest)
+    return body(hidden, *rest)
+
+
 def solution(mesh):
     placed = (
         P("walk", "elec", None),
@@ -195,7 +440,7 @@
         P("walk", "elec", None),
     )
     return jax.shard_map(
-        body,
+        any_body,
         mesh=mesh,
         in_specs=placed,
         out_specs=(P("walk", "elec", None), P("walk", "elec", None), P(), P(), P(), P()),

time: 326 us -> 178 us (0.55)
  local copies, waits for them, and re-layouts: 116 us -> 8.77 us
  matrix products: 35.7 us -> 0 us
  Pallas kernels: 0 us -> 20.6 us
  other arithmetic: 13.3 us -> 1.3 us
  waiting for transfers between devices: 139 us -> 132 us
  blocking collectives: 4.92 us -> 0 us
    dot_general x54 -> x0, matrix products: 35.7 us -> none  [the longest x2 10 us: place(): jnp.einsum('wsn,wsx->wnx', onehot, grouped, precision=lax.Precision.HIGHEST)]
    gather x24 -> x0, local copies, waits for them, and re-layouts: 27.3 us -> none  [the longest x12 20.4 us: slot_rows(): jnp.take(value_flat, flat_row, axis=0)]
    dynamic_slice x42 -> x0, local copies, waits for them, and re-layouts: 23.3 us -> none  [body(): lax.map(forward_item, (query_items, flat_slots, count_items))]
    reshape x28 -> x0, local copies, waits for them, and re-layouts: 21.4 us -> none  [the longest x24 11.1 us: split_heads(): array.reshape(array.shape[:-1] + (head_count, array.shape[-1] // head_cou...]
    pallas_call x0 -> x1, Pallas kernels: none -> 20.6 us  [pair_body(): pl.pallas_call(walker_kernel, out_shape=(jax.ShapeDtypeStruct(hidden.shap...]
    dynamic_update_slice x36 -> x0, local copies, waits for them, and re-layouts: 19.3 us -> none  [the longest x18 11 us: body(): lax.map(backward_item, (query_items, flat_slots, count_items, attended_it...]
    lt x12 -> x0, other arithmetic: 7.79 us -> none  [slot_rows(): jnp.arange(slot_count, dtype=jnp.int32) < live_count]
    select_n x24 -> x0, local copies, waits for them, and re-layouts: 7.77 us -> none  [the longest x12 3.88 us: slot_rows(): jnp.take(key_flat, flat_row, axis=0)]
  transfers between devices with their start and end apart: 3 -> 1, of which waited for: 2 -> 1; matrix products, arithmetic and copies ran while one was open for 6% -> 0% of each run, Pallas kernels for 0% -> 0%
where the time goes in v1:
time: 178 us; the launch traced here: 177 us
  waiting for transfers between devices  132 us (74%)
  Pallas kernels  20.6 us (12%)
  between operations  14.1 us (8%)
  local copies, waits for them, and re-layouts  8.77 us (5%)
    psum x1, waiting for transfers between devices, pair_body(): gw = lax.psum(gw, ('walk', 'elec')) / walkers_all  132 us
    pallas_call x1, Pallas kernels, pair_body(): pl.pallas_call(walker_kernel, out_shape=(jax.ShapeDtypeStruct(hidden.shap...  20.6 us
    unnamed x17, local copies, waits for them, and re-layouts  7.79 us
  transfers between devices with their start and end apart: 1, of which 1 were waited for; matrix products, arithmetic and copies ran while one was open for 0% of the time, Pallas kernels for 0%

profile of v1, /device:TPU:0, one launch (start us, length us, event | category | flops | bytes accessed | tf_op | source)
XLA Modules:
  0.0 177.2 jit_solution(14952574776657470020)
XLA Ops:
  7.2 0.0 copy-start.6
  7.2 0.0 all-reduce.2.cloned.1.call-start
  7.2 0.7 copy.14.nbr
  7.9 0.0 copy-done.6
  7.9 0.0 copy-start
  7.9 1.0 copy-done
  8.9 0.0 copy-start.1
  8.9 1.0 copy-done.1
  9.9 0.0 copy-start.2
  9.9 0.9 copy-done.2
  10.8 0.0 copy-start.3
  10.8 0.9 copy-done.3
  11.7 0.0 copy-start.4
  11.7 0.9 copy-done.4
  12.6 0.0 copy-start.5
  12.6 0.9 copy-done.5
  13.5 20.6 %shard_map.127 = (bf16[2,384,256]{2,1,0:T(8,128)(2,1)S(1)}, bf16[2,384,256]{2,1,0:T(8,128)(2,1)S(1)}, f32[4,256,256]{2,1,0:T(8,128)}) custom-call(s32[2,3,6]{2,1,0:T(4,128)S(1)} %copy.14.nbr, s32[2,3]{1,0:T(2,128)S(1)} %copy-done.6, bf16[2,384,256]{2,1,0:T(8,128)(2,1)S(1)} %copy-done, bf16[2,384,256]{2,1,0:T(8,128)(2,1)S(1)} %copy-done.1, ...), custom_call_target="tpu_custom_call" | custom-call | tf_op jit(solution)/shard_map/pallas_call | solution.py:391
  34.2 0.0 all-reduce.2.cloned.1.call-update
  34.2 132.4 %all-reduce.2.cloned.1.call-done = f32[4,256,256]{2,1,0:T(8,128)} async-done(((f32[4,256,256]{2,1,0:T(8,128)}), f32[4,256,256]{2,1,0:T(8,128)}) %all-reduce.2.cloned.1.call-update) | async-done | bytes 1048592 | tf_op jit(solution)/shard_map/psum | solution.py:420
  166.6 1.3 broadcast_multiply_fusion
  167.9 1.0 slice_bitcast_fusion
  168.9 0.7 copy.18
  169.6 0.7 copy.19
Async XLA Ops:
  7.2 0.7 copy-start.6
  7.2 159.4 %all-reduce.2.cloned.1.call-start = ((), (), s32[]{:S(2)}) async-start(), calls=%async_computation | async-start | bytes 2097152 | tf_op jit(solution)/shard_map/psum | solution.py:420
  7.9 1.0 copy-start
  8.9 1.0 copy-start.1
  9.9 0.9 copy-start.2
  10.8 0.9 copy-start.3
  11.7 0.9 copy-start.4
  12.6 0.9 copy-start.5
Sparse Core Ops, SparseCore 0:
  34.3 132.2 all-reduce.1

commit v2 on v1

--- a/solution.py
+++ b/solution.py
@@ -207,10 +207,11 @@
 
 
 def walker_kernel(
-    nbr, cnt, hid, cot, wq, wk, wv, wo, out, grad, gw,
-    hs, cs, bs, bsend, q_s, k_s, v_s, da_s, kt_s, vt_s, dat_s,
+    nbr, cnt, hid, cot, wq_h, wk_h, wv_h, wo_h, out, grad, full,
+    wq, wk, wv, wo, hs, cs, bs, bsend, q_s, k_s, v_s, da_s, kt_s, vt_s, dat_s,
     at_s, att_s, dqt_s, dq_s, w_s, ds_s, qb_s, db_s, kp_s, vp_s, dk_s, dv_s, ht_s, osend, gsend,
-    send_sem, recv_sem, local_sem, osem_s, osem_r,
+    g_s, a_s, r0, s1, b1, r1, s2, b2, r2, agz, agxy,
+    send_sem, recv_sem, local_sem, osem_s, osem_r, ar_send, ar_recv,
 ):
     e = lax.axis_index("elec")
     other = 1 - e
@@ -221,8 +222,32 @@
     rows = 2 * half
     pairs = hid.shape[2] // PAIR
 
+    walk = lax.axis_index("walk")
+    planes = lax.axis_size("walk") // 4
+    plane, spot = walk // 4, walk % 4
+    sx, sy = spot % 2, spot // 2
+    near = [((sy + r // 2) % 2) * 2 + (sx + r % 2) % 2 for r in range(1, 4)]
+    layers = [(plane + r) % planes for r in range(1, planes)]
+    spot_ids = [{"walk": plane * 4 + t, "elec": e} for t in near]
+    layer_ids = [{"walk": t * 4 + spot, "elec": e} for t in layers]
+    core_id = {"walk": walk, "elec": other}
+    mesh_ids = pl.DeviceIdType.MESH
+
     barrier = pltpu.get_barrier_semaphore()
-    pl.semaphore_signal(barrier, inc=1, device_id={"elec": other}, device_id_type=pl.DeviceIdType.MESH)
+    for peer in [core_id] + spot_ids + layer_ids:
+        pl.semaphore_signal(barrier, inc=1, device_id=peer, device_id_type=mesh_ids)
+
+    local = [
+        pltpu.make_async_copy(src, dst, local_sem.at[i])
+        for i, (src, dst) in enumerate(
+            (
+                (hid.at[e], hs.at[e]), (wq_h, wq), (wk_h, wk), (wv_h, wv),
+                (cot.at[e], cs.at[e]), (wo_h, wo),
+            )
+        )
+    ]
+    for copy in local:
+        copy.start()
 
     lane = lax.broadcasted_iota(jnp.int32, (16, 128), 1)
     sub = lax.broadcasted_iota(jnp.int32, (16, 128), 0)
@@ -234,7 +259,7 @@
                 bias = jnp.where((sub == a) & (lane == live), 0.0, bias)
         bsend[w] = bias.astype(BF16)
 
-    pl.semaphore_wait(barrier, 1)
+    pl.semaphore_wait(barrier, 3 + planes)
     sends = []
     for i, (src, dst) in enumerate(((hid, hs), (cot, cs), (bsend, bs))):
         copy = pltpu.make_async_remote_copy(
@@ -244,9 +269,9 @@
         copy.start()
         sends.append(copy)
 
-    hs[e] = hid[e]
-    cs[e] = cot[e]
     bs[e] = bsend[e]
+    for copy in local:
+        copy.wait()
 
     def project(h):
         rows_h = hs[h]
@@ -360,9 +385,6 @@
         sends.append(copy)
     out[e] = osend[e]
     grad[e] = gsend[e]
-    gw[0] = dot_nn(ht_s[...], d_query)
-    gw[1] = dot_nn(ht_s[...], d_key)
-    gw[2] = dot_nn(ht_s[...], d_value)
     at = jnp.concatenate(
         [
             jnp.concatenate([at_s[p, a] for a in range(n_blocks)], axis=1)
@@ -370,8 +392,88 @@
         ],
         axis=0,
     )
-    gw[3] = dot_nn(at, c_all)
+    parts = (
+        dot_nn(ht_s[...], d_query), dot_nn(ht_s[...], d_key),
+        dot_nn(ht_s[...], d_value), dot_nn(at, c_all),
+    )
+    width = hid.shape[2]
+    per = 4 * width // 2
+    for p in range(pairs):
+        for t, part in enumerate(parts):
+            g_s[p, t * width // per, pl.ds(t * width % per, width)] = part[:, p * PAIR : (p + 1) * PAIR]
+        a_s[p] = g_s[p].astype(BF16)
+
+    def transfers(stage, p):
+        if stage == 0:
+            todo = [(a_s.at[p, other], r0.at[p], core_id)]
+        elif stage == 1:
+            todo = [(b1.at[p, t], r1.at[p, r], spot_ids[r]) for r, t in enumerate(near)]
+        elif stage == 2:
+            todo = [(b2.at[p, t], r2.at[p, r], layer_ids[r]) for r, t in enumerate(layers)]
+        elif stage == 3:
+            todo = [(agz.at[p, plane], agz.at[p, plane], i) for i in layer_ids]
+        elif stage == 4:
+            todo = [(agxy.at[p, spot], agxy.at[p, spot], i) for i in spot_ids]
+        else:
+            todo = [(agxy.at[p], full.at[p, e], core_id)]
+        return [
+            pltpu.make_async_remote_copy(
+                src_ref=src, dst_ref=dst, send_sem=ar_send.at[stage, p, r],
+                recv_sem=ar_recv.at[stage, p, r], device_id=peer, device_id_type=mesh_ids,
+            )
+            for r, (src, dst, peer) in enumerate(todo)
+        ]
+
+    def begin(stage, p):
+        for copy in transfers(stage, p):
+            copy.start()
+
+    def finish(stage, p):
+        for copy in transfers(stage, p):
+            copy.wait()
+        if stage == 0:
+            s1[p] = (g_s[p, e] + r0[p].astype(F32)).reshape(s1.shape[1:])
+            b1[p] = s1[p].astype(BF16)
+        elif stage == 1:
+            total = s1[p, spot]
+            for r in range(3):
+                total = total + r1[p, r].astype(F32)
+            s2[p] = total.reshape(s2.shape[1:])
+            b2[p] = s2[p].astype(BF16)
+        elif stage == 2:
+            total = s2[p, plane]
+            for r in range(planes - 1):
+                total = total + r2[p, r].astype(F32)
+            agz[p, plane] = (total * (1.0 / (2 * lax.axis_size("walk")))).astype(BF16)
+        elif stage == 3:
+            agxy[p, spot] = agz[p]
+        elif stage == 4:
+            full[p, e] = agxy[p]
+
+    for p in range(pairs):
+        begin(0, p)
+    for stage in range(6):
+        for p in range(pairs):
+            finish(stage, p)
+            if stage < 5:
+                begin(stage + 1, p)
     for copy in sends:
+        copy.wait()
+
+
+def write_kernel(out, grad, full, out_h, grad_h, gq_h, gk_h, gv_h, go_h, gq, gk, gv, go, sem):
+    copies = [pltpu.make_async_copy(out, out_h, sem.at[0]), pltpu.make_async_copy(grad, grad_h, sem.at[1])]
+    for copy in copies:
+        copy.start()
+    width = gq.shape[0]
+    pairs = full.shape[0]
+    for t, (dst, dst_h) in enumerate(((gq, gq_h), (gk, gk_h), (gv, gv_h), (go, go_h))):
+        for p in range(pairs):
+            rows = full[p].reshape(4 * width, PAIR)[t * width : (t + 1) * width]
+            dst[:, p * PAIR : (p + 1) * PAIR] = rows.astype(F32)
+        copies.append(pltpu.make_async_copy(dst, dst_h, sem.at[2 + t]))
+        copies[-1].start()
+    for copy in copies:
         copy.wait()
 
 
@@ -381,6 +483,11 @@
     rows, pairs, n_blocks = 2 * half, width // PAIR, 2 * blocks
     vmem = pl.BlockSpec(memory_space=pltpu.VMEM)
     smem = pl.BlockSpec(memory_space=pltpu.SMEM)
+    hbm = pl.BlockSpec(memory_space=pltpu.HBM)
+    planes = lax.axis_size("walk") // 4
+    peers = max(3, planes - 1)
+    per = 4 * width // 2
+    fine = per // 4 // planes
     both = (2, half, width)
     by_pair = (pairs, 2, blocks, BLOCK, PAIR)
     by_pair2 = (pairs, 2, blocks, 2 * BLOCK, PAIR)
@@ -388,16 +495,17 @@
     def buf(*shape, dtype=BF16):
         return pltpu.VMEM(shape, dtype)
 
-    out, grad, gw = pl.pallas_call(
+    out, grad, full = pl.pallas_call(
         walker_kernel,
         out_shape=(
             jax.ShapeDtypeStruct(hidden.shape, BF16),
             jax.ShapeDtypeStruct(hidden.shape, BF16),
-            jax.ShapeDtypeStruct((4, width, width), F32),
+            jax.ShapeDtypeStruct((pairs, 2, 4, planes, fine, PAIR), BF16),
         ),
-        in_specs=[smem, smem] + [vmem] * 6,
+        in_specs=[smem, smem] + [hbm] * 6,
         out_specs=(vmem, vmem, vmem),
         scratch_shapes=[
+            buf(width, width), buf(width, width), buf(width, width), buf(width, width),
             buf(*both), buf(*both), buf(2, 16, 128), buf(2, 16, 128),
             buf(*both), buf(*both), buf(*both), buf(*both),
             buf(pairs, PAIR, rows), buf(pairs, PAIR, rows), buf(pairs, n_blocks, PAIR, BLOCK),
@@ -408,22 +516,38 @@
             buf(pairs, rows, 2 * PAIR), buf(pairs, rows, PAIR),
             buf(2, pairs, rows, PAIR), buf(2, pairs, rows, PAIR),
             buf(width, rows), buf(*both), buf(*both),
+            buf(pairs, 2, per, PAIR, dtype=F32), buf(pairs, 2, per, PAIR), buf(pairs, per, PAIR),
+            buf(pairs, 4, per // 4, PAIR, dtype=F32), buf(pairs, 4, per // 4, PAIR),
+            buf(pairs, 3, per // 4, PAIR),
+            buf(pairs, planes, fine, PAIR, dtype=F32), buf(pairs, planes, fine, PAIR),
+            buf(pairs, planes - 1, fine, PAIR),
+            buf(pairs, planes, fine, PAIR), buf(pairs, 4, planes, fine, PAIR),
             pltpu.SemaphoreType.DMA((3,)), pltpu.SemaphoreType.DMA((3,)),
-            pltpu.SemaphoreType.DMA((2,)),
+            pltpu.SemaphoreType.DMA((6,)),
             pltpu.SemaphoreType.DMA((2,)), pltpu.SemaphoreType.DMA((2,)),
+            pltpu.SemaphoreType.DMA((6, pairs, peers)), pltpu.SemaphoreType.DMA((6, pairs, peers)),
         ],
         compiler_params=pltpu.CompilerParams(
             collective_id=0, has_side_effects=True, vmem_limit_bytes=48 * 1024 * 1024
         ),
     )(neighbours, counts, hidden, cotangent, w_query, w_key, w_value, w_out)
-    walkers_all = hidden.shape[0] * lax.axis_size("walk")
-    gw = lax.psum(gw, ("walk", "elec")) / walkers_all
-    return out, grad, gw[0], gw[1], gw[2], gw[3]
+    grads = jax.ShapeDtypeStruct((width, width), F32)
+    return pl.pallas_call(
+        write_kernel,
+        out_shape=(
+            jax.ShapeDtypeStruct(hidden.shape, BF16), jax.ShapeDtypeStruct(hidden.shape, BF16),
+            grads, grads, grads, grads,
+        ),
+        in_specs=[pl.BlockSpec(memory_space=pl.ANY)] * 2 + [vmem],
+        out_specs=(hbm,) * 6,
+        scratch_shapes=[buf(width, width, dtype=F32)] * 4 + [pltpu.SemaphoreType.DMA((6,))],
+    )(out, grad, full)
 
 
 def any_body(hidden, *rest):
     blocks = rest[4].shape[1]
-    if lax.axis_size("elec") == 2 and hidden.shape[0] == 2 and 2 * blocks <= 128 and blocks <= 16:
+    fits = hidden.shape[0] == 2 and 2 * blocks <= 128 and blocks <= 16
+    if fits and lax.axis_size("elec") == 2 and lax.axis_size("walk") in (8, 16):
         return pair_body(hidden, *rest)
     return body(hidden, *rest)
 

time: 178 us -> 78.1 us (0.44)
  waiting for transfers between devices: 132 us -> 0 us
  Pallas kernels: 20.6 us -> 68.5 us
  between operations: 14.1 us -> 0.67 us
    psum x1 -> x0, waiting for transfers between devices: 132 us -> none  [pair_body(): gw = lax.psum(gw, ('walk', 'elec')) / walkers_all]
    pallas_call x0 -> x1, Pallas kernels: none -> 26 us  [pair_body(): pl.pallas_call(write_kernel, out_shape=(jax.ShapeDtypeStruct(hidden.shape...]
    pallas_call x1, Pallas kernels: 20.6 us -> 42.5 us  [pair_body(): pl.pallas_call(walker_kernel, out_shape=(jax.ShapeDtypeStruct(hidden.shap...]
    unnamed x17 -> x21, local copies, waits for them, and re-layouts: 7.79 us -> 8.59 us
  transfers between devices with their start and end apart: 1 -> 0, of which waited for: 1 -> 0; matrix products, arithmetic and copies ran while one was open for 0% -> 0% of each run, Pallas kernels for 0% -> 0%
where the time goes in v2:
time: 78.1 us; the launch traced here: 77.8 us
  Pallas kernels  68.5 us (88%)
  local copies, waits for them, and re-layouts  8.59 us (11%)
    pallas_call x1, Pallas kernels, pair_body(): pl.pallas_call(walker_kernel, out_shape=(jax.ShapeDtypeStruct(hidden.shap...  42.5 us
    pallas_call x1, Pallas kernels, pair_body(): pl.pallas_call(write_kernel, out_shape=(jax.ShapeDtypeStruct(hidden.shape...  26 us
    unnamed x21, local copies, waits for them, and re-layouts  8.59 us

profile of v2, /device:TPU:0, one launch (start us, length us, event | category | flops | bytes accessed | tf_op | source)
XLA Modules:
  0.0 77.8 jit_solution(17896536898806905068)
XLA Ops:
  0.6 0.0 copy-start.9
  0.6 0.7 copy.14.nbr
  1.3 0.0 copy-done.9
  1.3 0.0 copy-start.1
  1.3 1.0 %copy-done.1 = bf16[2,384,256]{2,1,0:T(8,128)(2,1)S(1)} copy-done((bf16[2,384,256]{2,1,0:T(8,128)(2,1)S(1)}, bf16[2,384,256]{2,1,0:T(8,128)(2,1)}, u32[]{:S(2)}) %copy-start.1) | copy-done | bytes 393240
  2.3 0.0 copy-start.2
  2.3 1.0 %copy-done.2 = bf16[2,384,256]{2,1,0:T(8,128)(2,1)S(1)} copy-done((bf16[2,384,256]{2,1,0:T(8,128)(2,1)S(1)}, bf16[2,384,256]{2,1,0:T(8,128)(2,1)}, u32[]{:S(2)}) %copy-start.2) | copy-done | bytes 393240
  3.3 0.0 copy-start.5
  3.3 0.9 %copy-done.5 = bf16[256,256]{1,0:T(8,128)(2,1)S(1)} copy-done((bf16[256,256]{1,0:T(8,128)(2,1)S(1)}, bf16[256,256]{1,0:T(8,128)(2,1)}, u32[]{:S(2)}) %copy-start.5) | copy-done | bytes 131096
  4.2 0.0 copy-start.6
  4.2 0.9 %copy-done.6 = bf16[256,256]{1,0:T(8,128)(2,1)S(1)} copy-done((bf16[256,256]{1,0:T(8,128)(2,1)S(1)}, bf16[256,256]{1,0:T(8,128)(2,1)}, u32[]{:S(2)}) %copy-start.6) | copy-done | bytes 131096
  5.1 0.0 copy-start.7
  5.1 0.9 %copy-done.7 = bf16[256,256]{1,0:T(8,128)(2,1)S(1)} copy-done((bf16[256,256]{1,0:T(8,128)(2,1)S(1)}, bf16[256,256]{1,0:T(8,128)(2,1)}, u32[]{:S(2)}) %copy-start.7) | copy-done | bytes 131096
  6.0 0.0 copy-start.8
  6.0 0.9 %copy-done.8 = bf16[256,256]{1,0:T(8,128)(2,1)S(1)} copy-done((bf16[256,256]{1,0:T(8,128)(2,1)S(1)}, bf16[256,256]{1,0:T(8,128)(2,1)}, u32[]{:S(2)}) %copy-start.8) | copy-done | bytes 131096
  6.9 42.5 %shard_map.127 = (bf16[2,384,256]{2,1,0:T(8,128)(2,1)S(1)}, bf16[2,384,256]{2,1,0:T(8,128)(2,1)S(1)}, bf16[2,2,4,4,32,128]{5,4,3,2,1,0:T(8,128)(2,1)S(1)}) custom-call(s32[2,3,6]{2,1,0:T(4,128)S(1)} %copy.14.nbr, s32[2,3]{1,0:T(2,128)S(1)} %copy-done.9, bf16[2,384,256]{2,1,0:T(8,128)(2,1)S(1)} %copy-done.1, bf16[2,384,256]{2,1,0:T(8,128)(2,1)S(1)} %copy-done.2, ...), custom_call_target="tpu_custom_call" | custom-call | tf_op jit(solution)/shard_map/pallas_call | solution.py:498
  49.4 0.0 copy-start
  49.4 0.8 %copy-done = bf16[2,2,4,4,32,128]{5,4,3,2,1,0:T(8,128)(2,1)} copy-done((bf16[2,2,4,4,32,128]{5,4,3,2,1,0:T(8,128)(2,1)}, bf16[2,2,4,4,32,128]{5,4,3,2,1,0:T(8,128)(2,1)S(1)}, u32[]{:S(2)}) %copy-start) | copy-done | bytes 524312
  50.2 0.0 copy-start.3
  50.2 0.7 copy-done.3
  51.0 0.0 copy-start.4
  51.0 0.8 copy-done.4
  51.7 26.0 %shard_map.128 = (bf16[2,384,256]{2,1,0:T(8,128)(2,1)}, bf16[2,384,256]{2,1,0:T(8,128)(2,1)}, f32[256,256]{1,0:T(8,128)}, f32[256,256]{1,0:T(8,128)}, f32[256,256]{1,0:T(8,128)}, /*index=5*/f32[256,256]{1,0:T(8,128)}) custom-call(bf16[2,384,256]{2,1,0:T(8,128)(2,1)} %copy-done.3, bf16[2,384,256]{2,1,0:T(8,128)(2,1)} %copy-done.4, ...), custom_call_target="tpu_custom_call" | custom-call | tf_op jit(solution)/shard_map/pallas_call | solution.py:535
Async XLA Ops:
  0.6 0.7 copy-start.9
  1.3 1.0 %copy-start.1 = (bf16[2,384,256]{2,1,0:T(8,128)(2,1)S(1)}, bf16[2,384,256]{2,1,0:T(8,128)(2,1)}, u32[]{:S(2)}) copy-start(bf16[2,384,256]{2,1,0:T(8,128)(2,1)} %hid.1) | copy-start | bytes 1179652
  2.3 1.0 %copy-start.2 = (bf16[2,384,256]{2,1,0:T(8,128)(2,1)S(1)}, bf16[2,384,256]{2,1,0:T(8,128)(2,1)}, u32[]{:S(2)}) copy-start(bf16[2,384,256]{2,1,0:T(8,128)(2,1)} %cot.1) | copy-start | bytes 1179652
  3.3 0.9 %copy-start.5 = (bf16[256,256]{1,0:T(8,128)(2,1)S(1)}, bf16[256,256]{1,0:T(8,128)(2,1)}, u32[]{:S(2)}) copy-start(bf16[256,256]{1,0:T(8,128)(2,1)} %wq_h.1) | copy-start | bytes 393220
  4.2 0.9 %copy-start.6 = (bf16[256,256]{1,0:T(8,128)(2,1)S(1)}, bf16[256,256]{1,0:T(8,128)(2,1)}, u32[]{:S(2)}) copy-start(bf16[256,256]{1,0:T(8,128)(2,1)} %wk_h.1) | copy-start | bytes 393220
  5.1 0.9 %copy-start.7 = (bf16[256,256]{1,0:T(8,128)(2,1)S(1)}, bf16[256,256]{1,0:T(8,128)(2,1)}, u32[]{:S(2)}) copy-start(bf16[256,256]{1,0:T(8,128)(2,1)} %wv_h.1) | copy-start | bytes 393220
  6.0 0.9 %copy-start.8 = (bf16[256,256]{1,0:T(8,128)(2,1)S(1)}, bf16[256,256]{1,0:T(8,128)(2,1)}, u32[]{:S(2)}) copy-start(bf16[256,256]{1,0:T(8,128)(2,1)} %wo_h.1) | copy-start | bytes 393220
  49.4 0.8 %copy-start = (bf16[2,2,4,4,32,128]{5,4,3,2,1,0:T(8,128)(2,1)}, bf16[2,2,4,4,32,128]{5,4,3,2,1,0:T(8,128)(2,1)S(1)}, u32[]{:S(2)}) copy-start(bf16[2,2,4,4,32,128]{5,4,3,2,1,0:T(8,128)(2,1)S(1)} %get-tuple-element.11.full) | copy-start | bytes 1572868
  50.2 0.7 copy-start.3
  51.0 0.8 copy-start.4

commit v3 on v2

--- a/solution.py
+++ b/solution.py
@@ -308,9 +308,9 @@
             qb_s[p, a // blocks, a % blocks] = by_head(q_s[a // blocks, r, lanes])
             db_s[p, a // blocks, a % blocks] = by_head(da_s[a // blocks, r, lanes])
 
-    def group(step, carry):
-        p = step // 2
-        g = step % 2
+    ht_s[...] = hs[...].reshape(rows, -1).T
+
+    def group(p, g, hooks=None):
         for i in range(blocks):
             a = g * blocks + i
             q2 = qb_s[p, g, i]
@@ -342,70 +342,30 @@
             dqt = (dqt * HD ** (-0.5)).astype(BF16)
             dqt_s[p, a] = dqt
             dq_s[p, g, i] = dqt.T
+            if hooks and hooks[i]:
+                hooks[i]()
         dk_s[g, p] = dot_nn(ds_s[...], qb_s[p, g].reshape(-1, PAIR)).astype(BF16)
         dv_s[g, p] = dot_nn(w_s[...], db_s[p, g].reshape(-1, PAIR)).astype(BF16)
-        return carry
-
-    lax.fori_loop(0, 2 * pairs, group, 0)
-
-    def whole(ref):
-        return jnp.concatenate([ref[p].reshape(rows, PAIR) for p in range(pairs)], axis=1)
-
-    h_all = hs[...].reshape(rows, -1)
-    c_all = cs[...].reshape(rows, -1)
-    ht = h_all.T
-    ht_s[...] = ht
-
-    def summed(ref):
-        return jnp.concatenate(
-            [(ref[0, p].astype(F32) + ref[1, p].astype(F32)).astype(BF16) for p in range(pairs)],
-            axis=1,
-        )
-
-    attended = whole(att_s)
-    d_query = whole(dq_s)
-    d_key = summed(dk_s)
-    d_value = summed(dv_s)
-    result = (h_all.astype(F32) + dot_nn(attended, wo[...])).astype(BF16)
-    osend[...] = result.reshape(osend.shape)
-    back = (
-        c_all.astype(F32)
-        + dot_nt(d_query, wq[...])
-        + dot_nt(d_key, wk[...])
-        + dot_nt(d_value, wv[...])
-    ).astype(BF16)
-    gsend[...] = back.reshape(gsend.shape)
-    sends = []
-    for i, (src, dst) in enumerate(((osend, out), (gsend, grad))):
-        copy = pltpu.make_async_remote_copy(
-            src_ref=src.at[other], dst_ref=dst.at[e], send_sem=osem_s.at[i], recv_sem=osem_r.at[i],
-            device_id={"elec": other}, device_id_type=pl.DeviceIdType.MESH,
-        )
-        copy.start()
-        sends.append(copy)
-    out[e] = osend[e]
-    grad[e] = gsend[e]
-    at = jnp.concatenate(
-        [
-            jnp.concatenate([at_s[p, a] for a in range(n_blocks)], axis=1)
-            for p in range(pairs)
-        ],
-        axis=0,
-    )
-    parts = (
-        dot_nn(ht_s[...], d_query), dot_nn(ht_s[...], d_key),
-        dot_nn(ht_s[...], d_value), dot_nn(at, c_all),
-    )
     width = hid.shape[2]
-    per = 4 * width // 2
-    for p in range(pairs):
-        for t, part in enumerate(parts):
-            g_s[p, t * width // per, pl.ds(t * width % per, width)] = part[:, p * PAIR : (p + 1) * PAIR]
-        a_s[p] = g_s[p].astype(BF16)
+
+    def summed(ref, p):
+        return (ref[0, p].astype(F32) + ref[1, p].astype(F32)).astype(BF16)
+
+    def weight_parts(p):
+        lower = g_s.at[p, 0]
+        upper = g_s.at[p, 1]
+        lower[:width] = dot_nn(ht_s[...], dq_s[p].reshape(rows, PAIR))
+        lower[width:] = dot_nn(ht_s[...], summed(dk_s, p))
+        upper[:width] = dot_nn(ht_s[...], summed(dv_s, p))
+        at = jnp.concatenate([at_s[p, a] for a in range(n_blocks)], axis=1)
+        part = dot_nn(at, cs[...].reshape(rows, -1))
+        for c in range(pairs):
+            upper[pl.ds(width + c * PAIR, PAIR)] = part[:, c * PAIR : (c + 1) * PAIR]
+        a_s[p] = g_s[p, other].astype(BF16)
 
     def transfers(stage, p):
         if stage == 0:
-            todo = [(a_s.at[p, other], r0.at[p], core_id)]
+            todo = [(a_s.at[p], r0.at[p], core_id)]
         elif stage == 1:
             todo = [(b1.at[p, t], r1.at[p, r], spot_ids[r]) for r, t in enumerate(near)]
         elif stage == 2:
@@ -450,15 +410,59 @@
         elif stage == 4:
             full[p, e] = agxy[p]
 
-    for p in range(pairs):
-        begin(0, p)
-    for stage in range(6):
-        for p in range(pairs):
-            finish(stage, p)
-            if stage < 5:
-                begin(stage + 1, p)
+
+    def advance(stage, p):
+        finish(stage, p)
+        begin(stage + 1, p)
+
+    def first_pair(g, carry):
+        group(0, g)
+        return carry
+
+    lax.fori_loop(0, 2, first_pair, 0)
+    weight_parts(0)
+    begin(0, 0)
+    group(1, 0, [None, lambda: advance(0, 0), None])
+    group(1, 1, [lambda: advance(1, 0), None, lambda: advance(2, 0)])
+    weight_parts(1)
+    begin(0, 1)
+
+    def whole(ref):
+        return jnp.concatenate([ref[p].reshape(rows, PAIR) for p in range(pairs)], axis=1)
+
+    def give(i, src, dst):
+        copy = pltpu.make_async_remote_copy(
+            src_ref=src.at[other], dst_ref=dst.at[e], send_sem=osem_s.at[i], recv_sem=osem_r.at[i],
+            device_id=core_id, device_id_type=mesh_ids,
+        )
+        copy.start()
+        dst[e] = src[e]
+        return copy
+
+    result = (hs[...].reshape(rows, -1).astype(F32) + dot_nn(whole(att_s), wo[...])).astype(BF16)
+    osend[...] = result.reshape(osend.shape)
+    advance(0, 1)
+    advance(3, 0)
+    sends = [give(0, osend, out)]
+    d_key = jnp.concatenate([summed(dk_s, p) for p in range(pairs)], axis=1)
+    d_value = jnp.concatenate([summed(dv_s, p) for p in range(pairs)], axis=1)
+    back = (
+        cs[...].reshape(rows, -1).astype(F32)
+        + dot_nt(whole(dq_s), wq[...])
+        + dot_nt(d_key, wk[...])
+        + dot_nt(d_value, wv[...])
+    ).astype(BF16)
+    gsend[...] = back.reshape(gsend.shape)
+    advance(1, 1)
+    sends.append(give(1, gsend, grad))
+    advance(4, 0)
+    advance(2, 1)
+    advance(3, 1)
+    finish(5, 0)
+    advance(4, 1)
     for copy in sends:
         copy.wait()
+    finish(5, 1)
 
 
 def write_kernel(out, grad, full, out_h, grad_h, gq_h, gk_h, gv_h, go_h, gq, gk, gv, go, sem):
@@ -469,8 +473,12 @@
     pairs = full.shape[0]
     for t, (dst, dst_h) in enumerate(((gq, gq_h), (gk, gk_h), (gv, gv_h), (go, go_h))):
         for p in range(pairs):
-            rows = full[p].reshape(4 * width, PAIR)[t * width : (t + 1) * width]
-            dst[:, p * PAIR : (p + 1) * PAIR] = rows.astype(F32)
+            rows = full[p].reshape(4 * width, PAIR)[t * width : (t + 1) * width].astype(F32)
+            if t < 3:
+                dst[:, p * PAIR : (p + 1) * PAIR] = rows
+            else:
+                for c in range(pairs):
+                    dst[p * PAIR : (p + 1) * PAIR, c * PAIR : (c + 1) * PAIR] = rows[c * PAIR : (c + 1) * PAIR]
         copies.append(pltpu.make_async_copy(dst, dst_h, sem.at[2 + t]))
         copies[-1].start()
     for copy in copies:
@@ -516,7 +524,7 @@
             buf(pairs, rows, 2 * PAIR), buf(pairs, rows, PAIR),
             buf(2, pairs, rows, PAIR), buf(2, pairs, rows, PAIR),
             buf(width, rows), buf(*both), buf(*both),
-            buf(pairs, 2, per, PAIR, dtype=F32), buf(pairs, 2, per, PAIR), buf(pairs, per, PAIR),
+            buf(pairs, 2, per, PAIR, dtype=F32), buf(pairs, per, PAIR), buf(pairs, per, PAIR),
             buf(pairs, 4, per // 4, PAIR, dtype=F32), buf(pairs, 4, per // 4, PAIR),
             buf(pairs, 3, per // 4, PAIR),
             buf(pairs, planes, fine, PAIR, dtype=F32), buf(pairs, planes, fine, PAIR),
@@ -528,7 +536,7 @@
             pltpu.SemaphoreType.DMA((6, pairs, peers)), pltpu.SemaphoreType.DMA((6, pairs, peers)),
         ],
         compiler_params=pltpu.CompilerParams(
-            collective_id=0, has_side_effects=True, vmem_limit_bytes=48 * 1024 * 1024
+            collective_id=0, has_side_effects=True, vmem_limit_bytes=62 * 1024 * 1024 + 768 * 1024
         ),
     )(neighbours, counts, hidden, cotangent, w_query, w_key, w_value, w_out)
     grads = jax.ShapeDtypeStruct((width, width), F32)
@@ -538,7 +546,7 @@
             jax.ShapeDtypeStruct(hidden.shape, BF16), jax.ShapeDtypeStruct(hidden.shape, BF16),
             grads, grads, grads, grads,
         ),
-        in_specs=[pl.BlockSpec(memory_space=pl.ANY)] * 2 + [vmem],
+        in_specs=[vmem] * 3,
         out_specs=(hbm,) * 6,
         scratch_shapes=[buf(width, width, dtype=F32)] * 4 + [pltpu.SemaphoreType.DMA((6,))],
     )(out, grad, full)
@@ -546,7 +554,7 @@
 
 def any_body(hidden, *rest):
     blocks = rest[4].shape[1]
-    fits = hidden.shape[0] == 2 and 2 * blocks <= 128 and blocks <= 16
+    fits = hidden.shape[0] == 2 and hidden.shape[2] == 2 * PAIR and 2 * blocks <= 128 and blocks <= 16
     if fits and lax.axis_size("elec") == 2 and lax.axis_size("walk") in (8, 16):
         return pair_body(hidden, *rest)
     return body(hidden, *rest)

time: 78.1 us -> 51.2 us (0.66)
  Pallas kernels: 68.5 us -> 49 us
  local copies, waits for them, and re-layouts: 8.59 us -> 1.28 us
    pallas_call x1, Pallas kernels: 26 us -> 2.55 us  [pair_body(): pl.pallas_call(write_kernel, out_shape=(jax.ShapeDtypeStruct(hidden.shape...]
    unnamed x21 -> x1, local copies, waits for them, and re-layouts: 8.59 us -> 1.28 us
    pallas_call x1, Pallas kernels: 42.5 us -> 46.5 us  [pair_body(): pl.pallas_call(walker_kernel, out_shape=(jax.ShapeDtypeStruct(hidden.shap...]
where the time goes in v3:
time: 51.2 us; the launch traced here: 51 us
  Pallas kernels  49 us (96%)
  local copies, waits for them, and re-layouts  1.28 us (2%)
  between operations  0.64 us (1%)
    pallas_call x1, Pallas kernels, pair_body(): pl.pallas_call(walker_kernel, out_shape=(jax.ShapeDtypeStruct(hidden.shap...  46.5 us
    pallas_call x1, Pallas kernels, pair_body(): pl.pallas_call(write_kernel, out_shape=(jax.ShapeDtypeStruct(hidden.shape...  2.55 us
    unnamed x1, local copies, waits for them, and re-layouts  1.28 us

profile of v3, /device:TPU:0, one launch (start us, length us, event | category | flops | bytes accessed | tf_op | source)
XLA Modules:
  0.0 51.0 jit_solution(4578961087298989059)
XLA Ops:
  0.6 1.3 %copy.14.nbr = s32[2,3,6]{2,1,0:T(4,128)} copy(s32[2,3,6]{2,0,1:T(2,128)} %param.13) | data formatting | bytes 288 | tf_op args[5]
  1.9 46.5 %shard_map.127 = (bf16[2,384,256]{2,1,0:T(8,128)(2,1)}, bf16[2,384,256]{2,1,0:T(8,128)(2,1)}, bf16[2,2,4,4,32,128]{5,4,3,2,1,0:T(8,128)(2,1)}) custom-call(s32[2,3,6]{2,1,0:T(4,128)} %copy.14.nbr, s32[2,3]{1,0:T(2,128)} %cnt.1, bf16[2,384,256]{2,1,0:T(8,128)(2,1)} %hid.1, bf16[2,384,256]{2,1,0:T(8,128)(2,1)} %cot.1, bf16[256,256]{1,0:T(8,128)(2,1)} %wq_h.1, ...), custom_call_target="tpu_custom_call" | custom-call | tf_op jit(solution)/shard_map/pallas_call | solution.py:506
  48.4 2.6 %shard_map.128 = (bf16[2,384,256]{2,1,0:T(8,128)(2,1)}, bf16[2,384,256]{2,1,0:T(8,128)(2,1)}, f32[256,256]{1,0:T(8,128)}, f32[256,256]{1,0:T(8,128)}, f32[256,256]{1,0:T(8,128)}, /*index=5*/f32[256,256]{1,0:T(8,128)}) custom-call(bf16[2,384,256]{2,1,0:T(8,128)(2,1)} %get-tuple-element.9.out, bf16[2,384,256]{2,1,0:T(8,128)(2,1)} %get-tuple-element.10.grad, ...), custom_call_target="tpu_custom_call" | custom-call | tf_op jit(solution)/shard_map/pallas_call | solution.py:543

commit v4 on v3

--- a/solution.py
+++ b/solution.py
@@ -210,7 +210,7 @@
     nbr, cnt, hid, cot, wq_h, wk_h, wv_h, wo_h, out, grad, full,
     wq, wk, wv, wo, hs, cs, bs, bsend, q_s, k_s, v_s, da_s, kt_s, vt_s, dat_s,
     at_s, att_s, dqt_s, dq_s, w_s, ds_s, qb_s, db_s, kp_s, vp_s, dk_s, dv_s, ht_s, osend, gsend,
-    g_s, a_s, r0, s1, b1, r1, s2, b2, r2, agz, agxy,
+    g_s, a_s, r0, s1, b1, r1, zall, agxy,
     send_sem, recv_sem, local_sem, osem_s, osem_r, ar_send, ar_recv,
 ):
     e = lax.axis_index("elec")
@@ -255,7 +255,7 @@
         bias = jnp.full((16, 128), NEG_FILL, F32)
         for a in range(blocks):
             for j in range(slots):
-                live = jnp.where(j < cnt[w, a], nbr[w, a, j], -1)
+                live = jnp.where(j < cnt[w, a], nbr[a, w, j], -1)
                 bias = jnp.where((sub == a) & (lane == live), 0.0, bias)
         bsend[w] = bias.astype(BF16)
 
@@ -369,10 +369,8 @@
         elif stage == 1:
             todo = [(b1.at[p, t], r1.at[p, r], spot_ids[r]) for r, t in enumerate(near)]
         elif stage == 2:
-            todo = [(b2.at[p, t], r2.at[p, r], layer_ids[r]) for r, t in enumerate(layers)]
+            todo = [(zall.at[p, plane], zall.at[p, plane], i) for i in layer_ids]
         elif stage == 3:
-            todo = [(agz.at[p, plane], agz.at[p, plane], i) for i in layer_ids]
-        elif stage == 4:
             todo = [(agxy.at[p, spot], agxy.at[p, spot], i) for i in spot_ids]
         else:
             todo = [(agxy.at[p], full.at[p, e], core_id)]
@@ -398,18 +396,14 @@
             total = s1[p, spot]
             for r in range(3):
                 total = total + r1[p, r].astype(F32)
-            s2[p] = total.reshape(s2.shape[1:])
-            b2[p] = s2[p].astype(BF16)
+            zall[p, plane] = total.astype(BF16)
         elif stage == 2:
-            total = s2[p, plane]
-            for r in range(planes - 1):
-                total = total + r2[p, r].astype(F32)
-            agz[p, plane] = (total * (1.0 / (2 * lax.axis_size("walk")))).astype(BF16)
+            total = zall[p, 0].astype(F32)
+            for r in range(1, planes):
+                total = total + zall[p, r].astype(F32)
+            agxy[p, spot] = (total * (1.0 / (2 * lax.axis_size("walk")))).astype(BF16)
         elif stage == 3:
-            agxy[p, spot] = agz[p]
-        elif stage == 4:
             full[p, e] = agxy[p]
-
 
     def advance(stage, p):
         finish(stage, p)
@@ -455,14 +449,12 @@
     gsend[...] = back.reshape(gsend.shape)
     advance(1, 1)
     sends.append(give(1, gsend, grad))
-    advance(4, 0)
+    finish(4, 0)
     advance(2, 1)
     advance(3, 1)
-    finish(5, 0)
-    advance(4, 1)
     for copy in sends:
         copy.wait()
-    finish(5, 1)
+    finish(4, 1)
 
 
 def write_kernel(out, grad, full, out_h, grad_h, gq_h, gk_h, gv_h, go_h, gq, gk, gv, go, sem):
@@ -495,7 +487,6 @@
     planes = lax.axis_size("walk") // 4
     peers = max(3, planes - 1)
     per = 4 * width // 2
-    fine = per // 4 // planes
     both = (2, half, width)
     by_pair = (pairs, 2, blocks, BLOCK, PAIR)
     by_pair2 = (pairs, 2, blocks, 2 * BLOCK, PAIR)
@@ -508,7 +499,7 @@
         out_shape=(
             jax.ShapeDtypeStruct(hidden.shape, BF16),
             jax.ShapeDtypeStruct(hidden.shape, BF16),
-            jax.ShapeDtypeStruct((pairs, 2, 4, planes, fine, PAIR), BF16),
+            jax.ShapeDtypeStruct((pairs, 2, 4, per // 4, PAIR), BF16),
         ),
         in_specs=[smem, smem] + [hbm] * 6,
         out_specs=(vmem, vmem, vmem),
@@ -527,18 +518,16 @@
             buf(pairs, 2, per, PAIR, dtype=F32), buf(pairs, per, PAIR), buf(pairs, per, PAIR),
             buf(pairs, 4, per // 4, PAIR, dtype=F32), buf(pairs, 4, per // 4, PAIR),
             buf(pairs, 3, per // 4, PAIR),
-            buf(pairs, planes, fine, PAIR, dtype=F32), buf(pairs, planes, fine, PAIR),
-            buf(pairs, planes - 1, fine, PAIR),
-            buf(pairs, planes, fine, PAIR), buf(pairs, 4, planes, fine, PAIR),
+            buf(pairs, planes, per // 4, PAIR), buf(pairs, 4, per // 4, PAIR),
             pltpu.SemaphoreType.DMA((3,)), pltpu.SemaphoreType.DMA((3,)),
             pltpu.SemaphoreType.DMA((6,)),
             pltpu.SemaphoreType.DMA((2,)), pltpu.SemaphoreType.DMA((2,)),
-            pltpu.SemaphoreType.DMA((6, pairs, peers)), pltpu.SemaphoreType.DMA((6, pairs, peers)),
+            pltpu.SemaphoreType.DMA((5, pairs, peers)), pltpu.SemaphoreType.DMA((5, pairs, peers)),
         ],
         compiler_params=pltpu.CompilerParams(
             collective_id=0, has_side_effects=True, vmem_limit_bytes=62 * 1024 * 1024 + 768 * 1024
         ),
-    )(neighbours, counts, hidden, cotangent, w_query, w_key, w_value, w_out)
+    )(neighbours.transpose(1, 0, 2), counts, hidden, cotangent, w_query, w_key, w_value, w_out)
     grads = jax.ShapeDtypeStruct((width, width), F32)
     return pl.pallas_call(
         write_kernel,

time: 51.2 us -> 48.3 us (0.943)
  Pallas kernels: 49 us -> 47.4 us
  local copies, waits for them, and re-layouts: 1.28 us -> 0 us
    pallas_call x1, Pallas kernels: 46.5 us -> 44.9 us  [pair_body(): pl.pallas_call(walker_kernel, out_shape=(jax.ShapeDtypeStruct(hidden.shap...]
    unnamed x1 -> x0, local copies, waits for them, and re-layouts: 1.28 us -> none
where the time goes in v4:
time: 48.3 us; the launch traced here: 48.1 us
  Pallas kernels  47.4 us (98%)
  between operations  0.64 us (1%)
    pallas_call x1, Pallas kernels, pair_body(): pl.pallas_call(walker_kernel, out_shape=(jax.ShapeDtypeStruct(hidden.shap...  44.9 us
    pallas_call x1, Pallas kernels, pair_body(): pl.pallas_call(write_kernel, out_shape=(jax.ShapeDtypeStruct(hidden.shape...  2.55 us

profile of v4, /device:TPU:0, one launch (start us, length us, event | category | flops | bytes accessed | tf_op | source)
XLA Modules:
  0.0 48.1 jit_solution(86110613505424813)
XLA Ops:
  0.6 44.9 %shard_map.127 = (bf16[2,384,256]{2,1,0:T(8,128)(2,1)}, bf16[2,384,256]{2,1,0:T(8,128)(2,1)}, bf16[2,2,4,128,128]{4,3,2,1,0:T(8,128)(2,1)}) custom-call(s32[3,2,6]{2,1,0:T(2,128)} %bitcast.1, s32[2,3]{1,0:T(2,128)} %cnt.1, bf16[2,384,256]{2,1,0:T(8,128)(2,1)} %hid.1, bf16[2,384,256]{2,1,0:T(8,128)(2,1)} %cot.1, bf16[256,256]{1,0:T(8,128)(2,1)} %wq_h.1, ...), custom_call_target="tpu_custom_call" | custom-call | tf_op jit(solution)/shard_map/pallas_call | solution.py:497
  45.5 2.6 %shard_map.128 = (bf16[2,384,256]{2,1,0:T(8,128)(2,1)}, bf16[2,384,256]{2,1,0:T(8,128)(2,1)}, f32[256,256]{1,0:T(8,128)}, f32[256,256]{1,0:T(8,128)}, f32[256,256]{1,0:T(8,128)}, /*index=5*/f32[256,256]{1,0:T(8,128)}) custom-call(bf16[2,384,256]{2,1,0:T(8,128)(2,1)} %get-tuple-element.9.out, bf16[2,384,256]{2,1,0:T(8,128)(2,1)} %get-tuple-element.10.grad, ...), custom_call_target="tpu_custom_call" | custom-call | tf_op jit(solution)/shard_map/pallas_call | solution.py:532
